TPU v7x, 32 devices: a whole 2x2x4 slice. The times are simulated.
32 devices in a mesh: parts: 2 (over y), row: 4 (over z), col: 4 (over x, core).
Axes of the slice: x: 2, y: 2, z: 4, core: 2. Of those that a mesh axis runs over, the one named last changes fastest.
Arguments:
- latent: bfloat16 [256, 128, 320], P(('parts', 'row'), 'col'), parts along dimension 0, may hold values from -6 to 6
- hyper: bfloat16 [64, 32, 192], P(('parts', 'row'), 'col'), parts along dimension 0, may hold values from -6 to 6
- bounds: int32 [6], replicated, may hold values from 0 to 320, as said below
- hyper_weight: bfloat16 [3, 3, 192, 192], replicated, may hold values from -0.15625 to 0.15625
- prior_weight: bfloat16 [192, 640], replicated, may hold values from -0.4375 to 0.4375
- ctx_weight: bfloat16 [4, 320, 640], replicated, may hold values from -0.3125 to 0.3125
- chan_weight: bfloat16 [320, 640], replicated, may hold values from -0.3125 to 0.3125
- out_weight: bfloat16 [640, 640], replicated, may hold values from -0.25 to 0.25
Outputs:
- rate_map: float32 [256, 128], P(('parts', 'row'), 'col'), parts along dimension 0
- grad_latent: bfloat16 [256, 128, 320], P(('parts', 'row'), 'col'), parts along dimension 0
- grad_hyper: float32 [64, 32, 192], P(('parts', 'row'), 'col'), parts along dimension 0
There are 2 independent parts, one for each index of `parts`. A program takes and returns all parts, laid end to end along the dimension named above; an argument that names none is the same for every part. Nothing has to cross between parts.
Inputs may be any that keep to these rules, and one draw needn't show every extreme that they name: bounds[0] is 0, bounds[5] is 320, and bounds rises strictly.
All inputs are finite; a program needn't handle non-finite values.
Results may differ from a plain program's by a relative error of at most 0.0061.
Values may be sent and summed in bfloat16 or wider, within the bound.
A program may use at most 64 MiB of HBM per device.

v0:
```python
import jax
import jax.numpy as jnp
from jax import lax
from jax.sharding import PartitionSpec as P


def padded(cells, sides, width):
    for axis, dim in sides:
        count = lax.axis_size(axis)
        ends = count - 1
        head = lax.slice_in_dim(cells, 0, width, axis=dim)
        tail = lax.slice_in_dim(cells, cells.shape[dim] - width, cells.shape[dim], axis=dim)
        cells = jnp.concatenate(
            [
                lax.ppermute(tail, axis, [(i, (i + 1) % count) for i in range(ends)]),
                cells,
                lax.ppermute(head, axis, [((i + 1) % count, i) for i in range(ends)]),
            ],
            axis=dim,
        )
    return cells


def slice_ids(bounds, channels):
    chan = jnp.arange(channels, dtype=jnp.int32)
    ids = jnp.zeros((channels,), jnp.int32)
    for g in range(1, 5):
        ids = ids + (chan >= bounds[g]).astype(jnp.int32)
    return ids


def silu_grad(value):
    sig = jax.nn.sigmoid(value)
    return sig * (1.0 + value * (1.0 - sig))


def local(latent, hyper, bounds, hyper_weight, prior_weight, ctx_weight, chan_weight, out_weight):
    rows, cols, channels = latent.shape
    zrows, zcols, zch = hyper.shape
    hidden_units = prior_weight.shape[1]
    row_start = lax.axis_index("row") * rows
    col_start = lax.axis_index("col") * cols
    ids = slice_ids(bounds, channels)
    hid_ids = jnp.tile(ids, hidden_units // channels)
    par_ids = jnp.tile(ids, 2)
    same_mask = (ids[:, None] == hid_ids[None, :]).astype(jnp.bfloat16)
    prev_mask = (ids[:, None] < hid_ids[None, :]).astype(jnp.bfloat16)
    out_mask = (hid_ids[:, None] == par_ids[None, :]).astype(jnp.bfloat16)
    ctx_masked = ctx_weight * same_mask[None]
    chan_masked = chan_weight * prev_mask
    out_masked = out_weight * out_mask
    zpad = padded(hyper, (("row", 0), ("col", 1)), 1)
    taps = jnp.concatenate(
        [zpad[a : a + zrows, b : b + zcols] for a in range(3) for b in range(3)], axis=-1
    )
    hz = jnp.dot(
        taps.reshape(-1, 9 * zch),
        hyper_weight.reshape(9 * zch, zch),
        preferred_element_type=jnp.float32,
    )
    hfeat = jax.nn.silu(hz).astype(jnp.bfloat16)
    prior = jnp.dot(hfeat, prior_weight, preferred_element_type=jnp.float32).reshape(
        zrows, zcols, hidden_units
    )
    rows_idx = row_start + jnp.arange(rows, dtype=jnp.int32)
    cols_idx = col_start + jnp.arange(cols, dtype=jnp.int32)
    anchor = (rows_idx[:, None] + cols_idx[None, :]) % 2 == 0
    ya = jnp.where(anchor[..., None], latent, jnp.zeros_like(latent))
    ypad = padded(ya, (("row", 0), ("col", 1)), 1)
    stacked = jnp.stack(
        [ypad[0:rows, 1:-1], ypad[2:, 1:-1], ypad[1:-1, 0:cols], ypad[1:-1, 2:]], axis=2
    )
    stacked = stacked.reshape(-1, 4, channels)
    ctx = jnp.einsum("nkc,kch->nh", stacked, ctx_masked, preferred_element_type=jnp.float32)
    flat = latent.reshape(-1, channels)
    local_pre = ctx + jnp.dot(flat, chan_masked, preferred_element_type=jnp.float32)
    pre = local_pre.reshape(zrows, 4, zcols, 4, hidden_units) + prior[:, None, :, None, :]
    pre = pre.reshape(-1, hidden_units)
    hidden = jax.nn.silu(pre).astype(jnp.bfloat16)
    par = jnp.dot(hidden, out_masked, preferred_element_type=jnp.float32)
    mu = par[:, :channels]
    sraw = par[:, channels:]
    sigma = 0.11 + jax.nn.softplus(sraw)
    resid = (flat.astype(jnp.float32) - mu) / sigma
    nll = 0.5 * resid * resid + jnp.log(sigma)
    rate_map = jnp.mean(nll, axis=-1).reshape(rows, cols)
    g_mu = -resid / sigma
    g_sraw = (1.0 - resid * resid) / sigma * jax.nn.sigmoid(sraw)
    g_par = jnp.concatenate([g_mu, g_sraw], axis=-1).astype(jnp.bfloat16)
    g_hidden = jnp.dot(g_par, out_masked.T, preferred_element_type=jnp.float32)
    g_pre = (g_hidden * silu_grad(pre)).astype(jnp.bfloat16)
    g_grid = g_pre.reshape(rows, cols, hidden_units)
    gpad = padded(g_grid, (("row", 0), ("col", 1)), 1)
    gstack = jnp.stack(
        [gpad[2:, 1:-1], gpad[0:rows, 1:-1], gpad[1:-1, 2:], gpad[1:-1, 0:cols]], axis=2
    )
    gstack = gstack.reshape(-1, 4, hidden_units)
    spatial = jnp.einsum("nkh,kch->nc", gstack, ctx_masked, preferred_element_type=jnp.float32)
    chan_back = jnp.dot(g_pre, chan_masked.T, preferred_element_type=jnp.float32)
    anchor_flat = anchor.reshape(-1, 1).astype(jnp.float32)
    grad_latent = (resid / sigma + chan_back + anchor_flat * spatial).astype(jnp.bfloat16)
    grad_latent = grad_latent.reshape(rows, cols, channels)
    g_block = g_pre.astype(jnp.float32).reshape(zrows, 4, zcols, 4, hidden_units).sum(axis=(1, 3))
    g_h = jnp.dot(
        g_block.reshape(-1, hidden_units),
        prior_weight.T.astype(jnp.float32),
        precision=lax.Precision.HIGHEST,
    )
    g_hz = (g_h * silu_grad(hz)).astype(jnp.bfloat16).reshape(zrows, zcols, zch)
    gzpad = padded(g_hz, (("row", 0), ("col", 1)), 1)
    gtaps = jnp.stack(
        [gzpad[2 - a : 2 - a + zrows, 2 - b : 2 - b + zcols] for a in range(3) for b in range(3)],
        axis=2,
    )
    gtaps = gtaps.reshape(-1, 9, zch)
    grad_hyper = jnp.einsum(
        "nkz,kcz->nc", gtaps, hyper_weight.reshape(9, zch, zch), preferred_element_type=jnp.float32
    )
    grad_hyper = grad_hyper.reshape(zrows, zcols, zch)
    return (rate_map, grad_latent, grad_hyper)


def solution(mesh):
    in_specs = (
        P(("parts", "row"), "col", None),
        P(("parts", "row"), "col", None),
        P(),
        P(),
        P(),
        P(),
        P(),
        P(),
    )
    out_specs = (
        P(("parts", "row"), "col"),
        P(("parts", "row"), "col", None),
        P(("parts", "row"), "col", None),
    )
    return jax.shard_map(local, mesh=mesh, in_specs=in_specs, out_specs=out_specs, check_vma=False)
```

profile of v0, /device:TPU:1, one launch (start us, length us, event | category | flops | bytes accessed | tf_op | source)
XLA Modules:
  0.0 102.4 jit_solution(5439079413353268405)
XLA Ops:
  1.5 4.0 %collective-permute-start.4 = (bf16[1,8,192]{2,1,0:T(8,128)(2,1)S(1)}, bf16[1,8,192]{2,1,0:T(8,128)(2,1)S(1)}, u32[]{:S(2)}, u32[]{:S(2)}) collective-permute-start(bf16[1,8,192]{2,1,0:T(8,128)(2,1)S(1)} %get-tuple-element.46), channel_id=1, source_target_pairs={{0,4},{4,8},{8,12},{1,5},{5,9},{9,13},{2,6},{6,10},{10,14},{3,7},{... | collective-permute-start | bytes 9224 | tf_op jit(solution)/shard_map/ppermute | solution.py:15
  5.6 1.3 %collective-permute-start.5 = (bf16[1,8,192]{2,1,0:T(8,128)(2,1)S(1)}, bf16[1,8,192]{2,1,0:T(8,128)(2,1)S(1)}, u32[]{:S(2)}, u32[]{:S(2)}) collective-permute-start(bf16[1,8,192]{2,1,0:T(8,128)(2,1)S(1)} %get-tuple-element.45), channel_id=1, source_target_pairs={{4,0},{8,4},{12,8},{5,1},{9,5},{13,9},{6,2},{10,6},{14,10},{7,3},{... | collective-permute-start | bytes 9224 | tf_op jit(solution)/shard_map/ppermute | solution.py:17
  7.0 1.3 %broadcast_select_fusion = bf16[32,32,320]{2,1,0:T(8,128)(2,1)S(1)} fusion(bf16[32,32,320]{2,1,0:T(8,128)(2,1)} %param.8, pred[32,32]{1,0:T(8,128)(4,1)S(1)} %fusion.64), kind=kLoop, calls=%fused_computation.66 | loop fusion | flops 327680 | bytes 1311744 | tf_op jit(solution)/shard_map/jit(_where)/select_n | solution.py:68
  8.3 4.0 %collective-permute-start = (bf16[1,32,320]{2,1,0:T(8,128)(2,1)S(1)}, bf16[1,32,320]{2,1,0:T(8,128)(2,1)S(1)}, u32[]{:S(2)}, u32[]{:S(2)}) collective-permute-start(bf16[1,32,320]{2,1,0:T(8,128)(2,1)S(1)} %get-tuple-element.23), channel_id=1, source_target_pairs={{0,4},{4,8},{8,12},{1,5},{5,9},{9,13},{2,6},{6,10},{10,14},{3,7},{... | collective-permute-start | bytes 61448 | tf_op jit(solution)/shard_map/ppermute | solution.py:15
  12.3 1.3 %collective-permute-start.1 = (bf16[1,32,320]{2,1,0:T(8,128)(2,1)S(1)}, bf16[1,32,320]{2,1,0:T(8,128)(2,1)S(1)}, u32[]{:S(2)}, u32[]{:S(2)}) collective-permute-start(bf16[1,32,320]{2,1,0:T(8,128)(2,1)S(1)} %get-tuple-element.24), channel_id=1, source_target_pairs={{4,0},{8,4},{12,8},{5,1},{9,5},{13,9},{6,2},{10,6},{14,10},{7,3},{... | collective-permute-start | bytes 61448 | tf_op jit(solution)/shard_map/ppermute | solution.py:17
  14.3 2.5 %convert_add_fusion = s32[320]{0:T(512)S(1)} fusion(s32[]{:T(128)} %bitcast.8, s32[]{:T(128)} %bitcast.7, s32[]{:T(128)} %bitcast.6, s32[]{:T(128)} %bitcast.5), kind=kLoop, calls=%fused_computation.140 | loop fusion | flops 3520 | bytes 1296 | tf_op jit(solution)/shard_map/add | solution.py:28
  17.8 2.5 %fusion.47 = f32[640,1024]{0,1:T(8,128)} fusion(bf16[1024,320]{1,0:T(8,128)(2,1)S(1)} %bitcast.110, bf16[320,640]{1,0:T(8,128)(2,1)S(1)} %copy-done.8, s32[640]{0:T(1024)S(1)} %eq.51, s32[320]{0:T(512)S(1)} %convert_add_fusion), kind=kOutput, calls=%fused_computation.70 | convolution fusion | flops 419840000 | bytes 3690240 | tf_op jit(solution)/shard_map/dot_general | solution.py:76
  20.5 4.5 %collective-permute-start.6 = (bf16[10,1,192]{2,1,0:T(2,128)(2,1)S(1)}, bf16[10,1,192]{2,1,0:T(2,128)(2,1)S(1)}, u32[]{:S(2)}, u32[]{:S(2)}) collective-permute-start(bf16[10,1,192]{2,1,0:T(2,128)(2,1)S(1)} %get-tuple-element.39), channel_id=1, source_target_pairs={{0,1},{1,2},{2,3},{4,5},{5,6},{6,7},{8,9},{9,10},{10,11},{12,13},{... | collective-permute-start | bytes 11528 | tf_op jit(solution)/shard_map/ppermute | solution.py:15
  25.1 1.9 %collective-permute-start.7 = (bf16[10,1,192]{2,1,0:T(2,128)(2,1)S(1)}, bf16[10,1,192]{2,1,0:T(2,128)(2,1)S(1)}, u32[]{:S(2)}, u32[]{:S(2)}) collective-permute-start(bf16[10,1,192]{2,1,0:T(2,128)(2,1)S(1)} %get-tuple-element.38), channel_id=1, source_target_pairs={{1,0},{2,1},{3,2},{5,4},{6,5},{7,6},{9,8},{10,9},{11,10},{13,12},{... | collective-permute-start | bytes 11528 | tf_op jit(solution)/shard_map/ppermute | solution.py:17
  28.7 1.3 %collective-permute-done.7 = bf16[10,1,192]{2,1,0:T(2,128)(2,1)S(1)} collective-permute-done((bf16[10,1,192]{2,1,0:T(2,128)(2,1)S(1)}, bf16[10,1,192]{2,1,0:T(2,128)(2,1)S(1)}, u32[]{:S(2)}, u32[]{:S(2)}) %collective-permute-start.7) | collective-permute-done | bytes 3872 | tf_op jit(solution)/shard_map/ppermute | solution.py:17
  31.4 2.3 %collective-permute-start.2 = (bf16[34,1,320]{2,1,0:T(2,128)(2,1)}, bf16[34,1,320]{2,1,0:T(2,128)(2,1)}, u32[]{:S(2)}, u32[]{:S(2)}) collective-permute-start(bf16[34,1,320]{2,1,0:T(2,128)(2,1)} %get-tuple-element.19), channel_id=1, source_target_pairs={{0,1},{1,2},{2,3},{4,5},{5,6},{6,7},{8,9},{9,10},{10,11},{12,13},{... | collective-permute-start | bytes 65288 | tf_op jit(solution)/shard_map/ppermute | solution.py:15
  33.7 2.8 %collective-permute-start.3 = (bf16[34,1,320]{2,1,0:T(2,128)(2,1)}, bf16[34,1,320]{2,1,0:T(2,128)(2,1)}, u32[]{:S(2)}, u32[]{:S(2)}) collective-permute-start(bf16[34,1,320]{2,1,0:T(2,128)(2,1)} %get-tuple-element.20), channel_id=1, source_target_pairs={{1,0},{2,1},{3,2},{5,4},{6,5},{7,6},{9,8},{10,9},{11,10},{13,12},{... | collective-permute-start | bytes 65288 | tf_op jit(solution)/shard_map/ppermute | solution.py:17
  37.3 2.0 %add.164 = f32[1024,640]{1,0:T(8,128)} reshape(f32[8,4,8,4,640]{4,3,2,1,0:T(4,128)S(1)} %add.163) | data formatting | bytes 5242880 | tf_op jit(solution)/shard_map/add | solution.py:77
  39.4 4.0 %pad_maximum_fusion.11 = (bf16[32,32,320]{2,1,0:T(8,128)(2,1)S(1)}, bf16[32,32,320]{2,1,0:T(8,128)(2,1)S(1)}, bf16[32,32,320]{2,1,0:T(8,128)(2,1)}, bf16[32,32,320]{2,1,0:T(8,128)(2,1)S(1)}) fusion(bf16[34,1,320]{2,1,0:T(2,128)(2,1)} %collective-permute-done.2, bf16[1,32,320]{2,1,0:T(8,128)(2,1)S(1)} %collective-permute-done.1, ...), kind=kLoop, calls=%fused_computation.61 | loop fusion | flops 7864320 | bytes 3361280 | tf_op jit(solution)/shard_map/concatenate | solution.py:13
  43.5 2.2 %copy.27 = bf16[1024,1,320]{0,2,1:T(8,128)(2,1)} copy(bf16[1024,1,320]{2,0,1:T(8,128)(2,1)} %bitcast.115) | data formatting | bytes 1310720 | tf_op jit(solution)/shard_map/stack | solution.py:70
  48.2 5.8 %fusion.16 = f32[1024,640]{1,0:T(8,128)S(1)} fusion(f32[1024,640]{1,0:T(8,128)} %add.164, f32[640,1024]{0,1:T(8,128)} %fusion.47, bf16[1024,1,320]{0,2,1:T(8,128)(2,1)S(1)} %copy.30, bf16[1024,1,320]{0,2,1:T(8,128)(2,1)} %copy.29, bf16[1024,1,320]{0,2,1:T(8,128)(2,1)} %copy.28, bf16[1024,1,320]{0,2,1:T(8,128)(2,1)S(1)} %copy-done.6, ...), kind=kOutput, calls=%fused_computation.18 | convolution fusion | flops 1683783680 | bytes 12533760 | tf_op jit(solution)/shard_map/nkc,kch->nh/dot_general | solution.py:74
  54.1 1.4 %fusion.39 = f32[1024,640]{0,1:T(8,128)S(1)} fusion(f32[1024,640]{1,0:T(8,128)S(1)} %fusion.16, bf16[640,640]{1,0:T(8,128)(2,1)S(1)} %copy-done.21, s32[640]{0:T(1024)S(1)} %copy-done.15), kind=kOutput, calls=%fused_computation.48 | convolution fusion | flops 842956800 | bytes 6064640 | tf_op jit(solution)/shard_map/dot_general | solution.py:80
  55.5 1.7 %divide_convert_fusion = (bf16[1024,320]{0,1:T(8,128)(2,1)S(1)}, bf16[1024,320]{0,1:T(8,128)(2,1)S(1)}, f32[1024]{0:T(1024)S(1)}) fusion(f32[1024,640]{0,1:T(8,128)S(1)} %fusion.39, bf16[1024,320]{0,1:T(8,128)(2,1)S(1)} %copy-done.5), kind=kLoop, calls=%fused_computation.47 | loop fusion | flops 8190976 | bytes 4591616 | tf_op jit(solution)/shard_map/convert.1
  57.2 1.7 %multiply_convert_fusion = bf16[1024,640]{1,0:T(8,128)(2,1)S(1)} fusion(f32[1024,640]{1,0:T(8,128)S(1)} %fusion.16, bf16[1024,320]{0,1:T(8,128)(2,1)S(1)} %get-tuple-element.7, bf16[1024,320]{0,1:T(8,128)(2,1)S(1)} %get-tuple-element.6, bf16[640,640]{1,0:T(8,128)(2,1)S(1)} %copy-done.21, s32[640]{0:T(1024)S(1)} %copy-done.15), kind=kOutput, calls=%fused_computation.19 | convolution fusion | flops 848199680 | bytes 6064640 | tf_op jit(solution)/shard_map/dot_general | solution.py:90
  58.9 1.9 %reshape.258 = f32[8,4,8,4,640]{4,3,2,1,0:T(4,128)} reshape(bf16[1024,640]{1,0:T(8,128)(2,1)S(1)} %multiply_convert_fusion) | data formatting | bytes 3932160 | tf_op jit(solution)/shard_map/reshape | solution.py:103
  60.8 2.6 %reduce_sum.19 = f32[8,8,640]{2,1,0:T(8,128)S(1)} reduce(f32[8,4,8,4,640]{4,3,2,1,0:T(4,128)} %reshape.258, f32[]{:T(128)} %constant.46.clone.1), dimensions={1,3}, to_apply=%region_1.2 | reduce | flops 614400 | bytes 2785284 | tf_op jit(solution)/shard_map/reduce_sum | solution.py:103
  63.3 1.4 %fusion.40 = bf16[64,192]{1,0:T(8,128)(2,1)S(1)} fusion(bf16[192,640]{1,0:T(8,128)(2,1)} %param.12, f32[8,8,640]{2,1,0:T(8,128)S(1)} %reduce_sum.19, f32[64,192]{1,0:T(8,128)S(1)} %copy-done.11), kind=kOutput, calls=%fused_computation.52 | convolution fusion | flops 94482432 | bytes 483328 | tf_op jit(solution)/shard_map/dot_general | solution.py:104
  64.7 4.3 %collective-permute-start.12 = (bf16[1,8,192]{2,1,0:T(8,128)(2,1)S(1)}, bf16[1,8,192]{2,1,0:T(8,128)(2,1)S(1)}, u32[]{:S(2)}, u32[]{:S(2)}) collective-permute-start(bf16[1,8,192]{2,1,0:T(8,128)(2,1)S(1)} %get-tuple-element.40), channel_id=1, source_target_pairs={{0,4},{4,8},{8,12},{1,5},{5,9},{9,13},{2,6},{6,10},{10,14},{3,7},{... | collective-permute-start | bytes 9224 | tf_op jit(solution)/shard_map/ppermute | solution.py:15
  69.0 1.3 %collective-permute-start.13 = (bf16[1,8,192]{2,1,0:T(8,128)(2,1)S(1)}, bf16[1,8,192]{2,1,0:T(8,128)(2,1)S(1)}, u32[]{:S(2)}, u32[]{:S(2)}) collective-permute-start(bf16[1,8,192]{2,1,0:T(8,128)(2,1)S(1)} %get-tuple-element.41), channel_id=1, source_target_pairs={{4,0},{8,4},{12,8},{5,1},{9,5},{13,9},{6,2},{10,6},{14,10},{7,3},{... | collective-permute-start | bytes 9224 | tf_op jit(solution)/shard_map/ppermute | solution.py:17
  72.2 5.2 %collective-permute-start.9 = (bf16[1,32,640]{2,1,0:T(8,128)(2,1)}, bf16[1,32,640]{2,1,0:T(8,128)(2,1)}, u32[]{:S(2)}, u32[]{:S(2)}) collective-permute-start(bf16[1,32,640]{2,1,0:T(8,128)(2,1)} %get-tuple-element.15), channel_id=1, source_target_pairs={{0,4},{4,8},{8,12},{1,5},{5,9},{9,13},{2,6},{6,10},{10,14},{3,7},{... | collective-permute-start | bytes 122888 | tf_op jit(solution)/shard_map/ppermute | solution.py:15
  77.5 2.0 %collective-permute-start.14 = (bf16[10,1,192]{2,1,0:T(2,128)(2,1)S(1)}, bf16[10,1,192]{2,1,0:T(2,128)(2,1)S(1)}, u32[]{:S(2)}, u32[]{:S(2)}) collective-permute-start(bf16[10,1,192]{2,1,0:T(2,128)(2,1)S(1)} %get-tuple-element.34), channel_id=1, source_target_pairs={{1,0},{2,1},{3,2},{5,4},{6,5},{7,6},{9,8},{10,9},{11,10},{13,12},{... | collective-permute-start | bytes 11528 | tf_op jit(solution)/shard_map/ppermute | solution.py:17
  79.5 3.8 %collective-permute-start.15 = (bf16[10,1,192]{2,1,0:T(2,128)(2,1)S(1)}, bf16[10,1,192]{2,1,0:T(2,128)(2,1)S(1)}, u32[]{:S(2)}, u32[]{:S(2)}) collective-permute-start(bf16[10,1,192]{2,1,0:T(2,128)(2,1)S(1)} %get-tuple-element.33), channel_id=1, source_target_pairs={{0,1},{1,2},{2,3},{4,5},{5,6},{6,7},{8,9},{9,10},{10,11},{12,13},{... | collective-permute-start | bytes 11528 | tf_op jit(solution)/shard_map/ppermute | solution.py:15
  85.1 1.9 %collective-permute-start.10 = (bf16[34,1,640]{2,1,0:T(2,128)(2,1)S(1)}, bf16[34,1,640]{2,1,0:T(2,128)(2,1)S(1)}, u32[]{:S(2)}, u32[]{:S(2)}) collective-permute-start(bf16[34,1,640]{2,1,0:T(2,128)(2,1)S(1)} %get-tuple-element.11), channel_id=1, source_target_pairs={{1,0},{2,1},{3,2},{5,4},{6,5},{7,6},{9,8},{10,9},{11,10},{13,12},{... | collective-permute-start | bytes 130568 | tf_op jit(solution)/shard_map/ppermute | solution.py:17
  87.0 4.1 %collective-permute-start.11 = (bf16[34,1,640]{2,1,0:T(2,128)(2,1)S(1)}, bf16[34,1,640]{2,1,0:T(2,128)(2,1)S(1)}, u32[]{:S(2)}, u32[]{:S(2)}) collective-permute-start(bf16[34,1,640]{2,1,0:T(2,128)(2,1)S(1)} %get-tuple-element.12), channel_id=1, source_target_pairs={{0,1},{1,2},{2,3},{4,5},{5,6},{6,7},{8,9},{9,10},{10,11},{12,13},{... | collective-permute-start | bytes 130568 | tf_op jit(solution)/shard_map/ppermute | solution.py:15
  92.6 5.1 %pad_maximum_fusion.3 = (bf16[32,32,640]{2,1,0:T(8,128)(2,1)S(1)}, bf16[32,32,640]{2,1,0:T(8,128)(2,1)S(1)}, bf16[32,32,640]{2,1,0:T(8,128)(2,1)S(1)}, bf16[32,32,640]{2,1,0:T(8,128)(2,1)S(1)}) fusion(bf16[34,1,640]{2,1,0:T(2,128)(2,1)S(1)} %collective-permute-done.10, bf16[1,32,640]{2,1,0:T(8,128)(2,1)S(1)} %collective-permute-done.8, ...), kind=kLoop, calls=%fused_computation.37 | loop fusion | flops 15728640 | bytes 6722560 | tf_op jit(solution)/shard_map/concatenate | solution.py:13
  97.8 2.0 %fusion.27 = f32[1024,320]{0,1:T(8,128)S(1)} fusion(bf16[4,320,640]{2,1,0:T(8,128)(2,1)S(1)} %copy-done.20, bf16[1024,1,640]{2,0,1:T(8,128)(2,1)S(1)} %bitcast.117, bf16[1024,1,640]{2,0,1:T(8,128)(2,1)S(1)} %bitcast.116, bf16[1024,1,640]{2,0,1:T(8,128)(2,1)S(1)} %bitcast.119, bf16[1024,1,640]{2,0,1:T(8,128)(2,1)S(1)} %bitcast.118, ...), kind=kOutput, calls=%fused_computation.29 | convolution fusion | flops 1686732800 | bytes 8605696 | tf_op jit(solution)/shard_map/nkh,kch->nc/dot_general | solution.py:98
  99.8 1.5 %fusion.32 = bf16[1024,320]{0,1:T(8,128)(2,1)S(1)} fusion(f32[1024,320]{0,1:T(8,128)S(1)} %fusion.27, bf16[1024,640]{1,0:T(8,128)(2,1)S(1)} %multiply_convert_fusion, f32[1024,640]{0,1:T(8,128)S(1)} %copy-done.4, bf16[1024,320]{0,1:T(8,128)(2,1)S(1)} %copy-done.5, bf16[320,640]{1,0:T(8,128)(2,1)S(1)} %copy-done.9, s32[640]{0:T(1024)S(1)} %copy-done.15, ...), kind=kOutput, calls=%fused_computation.30 | convolution fusion | flops 424427520 | bytes 6967040 | tf_op jit(solution)/shard_map/dot_general | solution.py:99
  (103 shorter events, 15.5 us)
Async XLA Ops:
  0.6 29.7 %copy-start = (bf16[3,3,192,192]{3,2,1,0:T(8,128)(2,1)S(1)}, bf16[3,3,192,192]{3,2,1,0:T(8,128)(2,1)}, u32[]{:S(2)}) copy-start(bf16[3,3,192,192]{3,2,1,0:T(8,128)(2,1)} %param.11) | copy-start | bytes 1990660
  0.6 17.1 %copy-start.2 = (bf16[32,32,320]{2,1,0:T(8,128)(2,1)S(1)}, bf16[32,32,320]{2,1,0:T(8,128)(2,1)}, u32[]{:S(2)}) copy-start(bf16[32,32,320]{2,1,0:T(8,128)(2,1)} %param.8) | copy-start | bytes 1966084
  0.7 13.0 %copy-start.18 = (s32[6]{0:T(128)S(1)}, s32[6]{0:T(128)}, u32[]{:S(2)}) copy-start(s32[6]{0:T(128)} %param.10) | copy-start | bytes 76
  0.7 17.1 %copy-start.8 = (bf16[320,640]{1,0:T(8,128)(2,1)S(1)}, bf16[320,640]{1,0:T(8,128)(2,1)}, u32[]{:S(2)}) copy-start(bf16[320,640]{1,0:T(8,128)(2,1)} %param.14) | copy-start | bytes 1228804
  1.5 18.9 %collective-permute-start.4 = (bf16[1,8,192]{2,1,0:T(8,128)(2,1)S(1)}, bf16[1,8,192]{2,1,0:T(8,128)(2,1)S(1)}, u32[]{:S(2)}, u32[]{:S(2)}) collective-permute-start(bf16[1,8,192]{2,1,0:T(8,128)(2,1)S(1)} %get-tuple-element.46), channel_id=1, source_target_pairs={{0,4},{4,8},{8,12},{1,5},{5,9},{9,13},{2,6},{6,10},{10,14},{3,7},{... | collective-permute-start | bytes 9224 | tf_op jit(solution)/shard_map/ppermute | solution.py:15
  5.6 14.9 %collective-permute-start.5 = (bf16[1,8,192]{2,1,0:T(8,128)(2,1)S(1)}, bf16[1,8,192]{2,1,0:T(8,128)(2,1)S(1)}, u32[]{:S(2)}, u32[]{:S(2)}) collective-permute-start(bf16[1,8,192]{2,1,0:T(8,128)(2,1)S(1)} %get-tuple-element.45), channel_id=1, source_target_pairs={{4,0},{8,4},{12,8},{5,1},{9,5},{13,9},{6,2},{10,6},{14,10},{7,3},{... | collective-permute-start | bytes 9224 | tf_op jit(solution)/shard_map/ppermute | solution.py:17
  8.3 22.3 %copy-start.1 = (bf16[32,32,320]{2,1,0:T(8,128)(2,1)}, bf16[32,32,320]{2,1,0:T(8,128)(2,1)S(1)}, u32[]{:S(2)}) copy-start(bf16[32,32,320]{2,1,0:T(8,128)(2,1)S(1)} %broadcast_select_fusion) | copy-start | bytes 1966084
  8.3 22.3 %collective-permute-start = (bf16[1,32,320]{2,1,0:T(8,128)(2,1)S(1)}, bf16[1,32,320]{2,1,0:T(8,128)(2,1)S(1)}, u32[]{:S(2)}, u32[]{:S(2)}) collective-permute-start(bf16[1,32,320]{2,1,0:T(8,128)(2,1)S(1)} %get-tuple-element.23), channel_id=1, source_target_pairs={{0,4},{4,8},{8,12},{1,5},{5,9},{9,13},{2,6},{6,10},{10,14},{3,7},{... | collective-permute-start | bytes 61448 | tf_op jit(solution)/shard_map/ppermute | solution.py:15
  12.3 18.3 %collective-permute-start.1 = (bf16[1,32,320]{2,1,0:T(8,128)(2,1)S(1)}, bf16[1,32,320]{2,1,0:T(8,128)(2,1)S(1)}, u32[]{:S(2)}, u32[]{:S(2)}) collective-permute-start(bf16[1,32,320]{2,1,0:T(8,128)(2,1)S(1)} %get-tuple-element.24), channel_id=1, source_target_pairs={{4,0},{8,4},{12,8},{5,1},{9,5},{13,9},{6,2},{10,6},{14,10},{7,3},{... | collective-permute-start | bytes 61448 | tf_op jit(solution)/shard_map/ppermute | solution.py:17
  16.7 3.6 %copy-start.16 = (s32[320]{0:T(512)}, s32[320]{0:T(512)S(1)}, u32[]{:S(2)}) copy-start(s32[320]{0:T(512)S(1)} %convert_add_fusion) | copy-start | bytes 3844
  16.8 3.5 %copy-start.14 = (s32[640]{0:T(1024)}, s32[640]{0:T(1024)S(1)}, u32[]{:S(2)}) copy-start(s32[640]{0:T(1024)S(1)} %eq.51) | copy-start | bytes 7684
  17.8 2.7 %copy-start.13 = (bf16[8,8,192]{2,1,0:T(8,128)(2,1)S(1)}, bf16[8,8,192]{2,1,0:T(8,128)(2,1)}, u32[]{:S(2)}) copy-start(bf16[8,8,192]{2,1,0:T(8,128)(2,1)} %param.9) | copy-start | bytes 73732
  20.5 8.2 %collective-permute-start.6 = (bf16[10,1,192]{2,1,0:T(2,128)(2,1)S(1)}, bf16[10,1,192]{2,1,0:T(2,128)(2,1)S(1)}, u32[]{:S(2)}, u32[]{:S(2)}) collective-permute-start(bf16[10,1,192]{2,1,0:T(2,128)(2,1)S(1)} %get-tuple-element.39), channel_id=1, source_target_pairs={{0,1},{1,2},{2,3},{4,5},{5,6},{6,7},{8,9},{9,10},{10,11},{12,13},{... | collective-permute-start | bytes 11528 | tf_op jit(solution)/shard_map/ppermute | solution.py:15
  25.1 5.0 %collective-permute-start.7 = (bf16[10,1,192]{2,1,0:T(2,128)(2,1)S(1)}, bf16[10,1,192]{2,1,0:T(2,128)(2,1)S(1)}, u32[]{:S(2)}, u32[]{:S(2)}) collective-permute-start(bf16[10,1,192]{2,1,0:T(2,128)(2,1)S(1)} %get-tuple-element.38), channel_id=1, source_target_pairs={{1,0},{2,1},{3,2},{5,4},{6,5},{7,6},{9,8},{10,9},{11,10},{13,12},{... | collective-permute-start | bytes 11528 | tf_op jit(solution)/shard_map/ppermute | solution.py:17
  28.7 7.8 %copy-start.12 = (bf16[192,640]{1,0:T(8,128)(2,1)S(1)}, bf16[192,640]{1,0:T(8,128)(2,1)}, u32[]{:S(2)}) copy-start(bf16[192,640]{1,0:T(8,128)(2,1)} %param.12) | copy-start | bytes 737284
  30.6 5.9 %copy-start.10 = (f32[64,192]{1,0:T(8,128)}, f32[64,192]{1,0:T(8,128)S(1)}, u32[]{:S(2)}) copy-start(f32[64,192]{1,0:T(8,128)S(1)} %fusion.44) | copy-start | bytes 147460
  31.4 8.0 %collective-permute-start.2 = (bf16[34,1,320]{2,1,0:T(2,128)(2,1)}, bf16[34,1,320]{2,1,0:T(2,128)(2,1)}, u32[]{:S(2)}, u32[]{:S(2)}) collective-permute-start(bf16[34,1,320]{2,1,0:T(2,128)(2,1)} %get-tuple-element.19), channel_id=1, source_target_pairs={{0,1},{1,2},{2,3},{4,5},{5,6},{6,7},{8,9},{9,10},{10,11},{12,13},{... | collective-permute-start | bytes 65288 | tf_op jit(solution)/shard_map/ppermute | solution.py:15
  33.7 5.8 %collective-permute-start.3 = (bf16[34,1,320]{2,1,0:T(2,128)(2,1)}, bf16[34,1,320]{2,1,0:T(2,128)(2,1)}, u32[]{:S(2)}, u32[]{:S(2)}) collective-permute-start(bf16[34,1,320]{2,1,0:T(2,128)(2,1)} %get-tuple-element.20), channel_id=1, source_target_pairs={{1,0},{2,1},{3,2},{5,4},{6,5},{7,6},{9,8},{10,9},{11,10},{13,12},{... | collective-permute-start | bytes 65288 | tf_op jit(solution)/shard_map/ppermute | solution.py:17
  48.2 5.8 %copy-start.15 = (s32[640]{0:T(1024)S(1)}, s32[640]{0:T(1024)}, u32[]{:S(2)}) copy-start(s32[640]{0:T(1024)} %copy-done.14) | copy-start | bytes 7684
  48.2 5.8 %copy-start.21 = (bf16[640,640]{1,0:T(8,128)(2,1)S(1)}, bf16[640,640]{1,0:T(8,128)(2,1)}, u32[]{:S(2)}) copy-start(bf16[640,640]{1,0:T(8,128)(2,1)} %param.15) | copy-start | bytes 2457604
  60.8 2.6 %copy-start.11 = (f32[64,192]{1,0:T(8,128)S(1)}, f32[64,192]{1,0:T(8,128)}, u32[]{:S(2)}) copy-start(f32[64,192]{1,0:T(8,128)} %copy-done.10) | copy-start | bytes 147460
  64.7 12.7 %collective-permute-start.12 = (bf16[1,8,192]{2,1,0:T(8,128)(2,1)S(1)}, bf16[1,8,192]{2,1,0:T(8,128)(2,1)S(1)}, u32[]{:S(2)}, u32[]{:S(2)}) collective-permute-start(bf16[1,8,192]{2,1,0:T(8,128)(2,1)S(1)} %get-tuple-element.40), channel_id=1, source_target_pairs={{0,4},{4,8},{8,12},{1,5},{5,9},{9,13},{2,6},{6,10},{10,14},{3,7},{... | collective-permute-start | bytes 9224 | tf_op jit(solution)/shard_map/ppermute | solution.py:15
  69.0 8.5 %collective-permute-start.13 = (bf16[1,8,192]{2,1,0:T(8,128)(2,1)S(1)}, bf16[1,8,192]{2,1,0:T(8,128)(2,1)S(1)}, u32[]{:S(2)}, u32[]{:S(2)}) collective-permute-start(bf16[1,8,192]{2,1,0:T(8,128)(2,1)S(1)} %get-tuple-element.41), channel_id=1, source_target_pairs={{4,0},{8,4},{12,8},{5,1},{9,5},{13,9},{6,2},{10,6},{14,10},{7,3},{... | collective-permute-start | bytes 9224 | tf_op jit(solution)/shard_map/ppermute | solution.py:17
  70.9 13.3 %collective-permute-start.8 = (bf16[1,32,640]{2,1,0:T(8,128)(2,1)}, bf16[1,32,640]{2,1,0:T(8,128)(2,1)S(1)}, u32[]{:S(2)}, u32[]{:S(2)}) collective-permute-start(bf16[1,32,640]{2,1,0:T(8,128)(2,1)} %get-tuple-element.16), channel_id=1, source_target_pairs={{4,0},{8,4},{12,8},{5,1},{9,5},{13,9},{6,2},{10,6},{14,10},{7,3},{... | collective-permute-start | bytes 122888 | tf_op jit(solution)/shard_map/ppermute | solution.py:17
  72.2 12.0 %collective-permute-start.9 = (bf16[1,32,640]{2,1,0:T(8,128)(2,1)}, bf16[1,32,640]{2,1,0:T(8,128)(2,1)}, u32[]{:S(2)}, u32[]{:S(2)}) collective-permute-start(bf16[1,32,640]{2,1,0:T(8,128)(2,1)} %get-tuple-element.15), channel_id=1, source_target_pairs={{0,4},{4,8},{8,12},{1,5},{5,9},{9,13},{2,6},{6,10},{10,14},{3,7},{... | collective-permute-start | bytes 122888 | tf_op jit(solution)/shard_map/ppermute | solution.py:15
  77.5 6.5 %collective-permute-start.14 = (bf16[10,1,192]{2,1,0:T(2,128)(2,1)S(1)}, bf16[10,1,192]{2,1,0:T(2,128)(2,1)S(1)}, u32[]{:S(2)}, u32[]{:S(2)}) collective-permute-start(bf16[10,1,192]{2,1,0:T(2,128)(2,1)S(1)} %get-tuple-element.34), channel_id=1, source_target_pairs={{1,0},{2,1},{3,2},{5,4},{6,5},{7,6},{9,8},{10,9},{11,10},{13,12},{... | collective-permute-start | bytes 11528 | tf_op jit(solution)/shard_map/ppermute | solution.py:17
  79.5 4.5 %collective-permute-start.15 = (bf16[10,1,192]{2,1,0:T(2,128)(2,1)S(1)}, bf16[10,1,192]{2,1,0:T(2,128)(2,1)S(1)}, u32[]{:S(2)}, u32[]{:S(2)}) collective-permute-start(bf16[10,1,192]{2,1,0:T(2,128)(2,1)S(1)} %get-tuple-element.33), channel_id=1, source_target_pairs={{0,1},{1,2},{2,3},{4,5},{5,6},{6,7},{8,9},{9,10},{10,11},{12,13},{... | collective-permute-start | bytes 11528 | tf_op jit(solution)/shard_map/ppermute | solution.py:15
  85.1 7.1 %collective-permute-start.10 = (bf16[34,1,640]{2,1,0:T(2,128)(2,1)S(1)}, bf16[34,1,640]{2,1,0:T(2,128)(2,1)S(1)}, u32[]{:S(2)}, u32[]{:S(2)}) collective-permute-start(bf16[34,1,640]{2,1,0:T(2,128)(2,1)S(1)} %get-tuple-element.11), channel_id=1, source_target_pairs={{1,0},{2,1},{3,2},{5,4},{6,5},{7,6},{9,8},{10,9},{11,10},{13,12},{... | collective-permute-start | bytes 130568 | tf_op jit(solution)/shard_map/ppermute | solution.py:17
  87.0 5.6 %collective-permute-start.11 = (bf16[34,1,640]{2,1,0:T(2,128)(2,1)S(1)}, bf16[34,1,640]{2,1,0:T(2,128)(2,1)S(1)}, u32[]{:S(2)}, u32[]{:S(2)}) collective-permute-start(bf16[34,1,640]{2,1,0:T(2,128)(2,1)S(1)} %get-tuple-element.12), channel_id=1, source_target_pairs={{0,1},{1,2},{2,3},{4,5},{5,6},{6,7},{8,9},{9,10},{10,11},{12,13},{... | collective-permute-start | bytes 130568 | tf_op jit(solution)/shard_map/ppermute | solution.py:15
  92.2 5.6 %copy-start.19 = (f32[1024]{0:T(1024)S(1)}, f32[1024]{0:T(1024)}, u32[]{:S(2)}) copy-start(f32[1024]{0:T(1024)} %fusion.67) | copy-start | bytes 12292
  92.2 5.6 %copy-start.20 = (bf16[4,320,640]{2,1,0:T(8,128)(2,1)S(1)}, bf16[4,320,640]{2,1,0:T(8,128)(2,1)}, u32[]{:S(2)}) copy-start(bf16[4,320,640]{2,1,0:T(8,128)(2,1)} %param.13) | copy-start | bytes 4915204
  97.8 2.0 %copy-start.4 = (f32[1024,640]{0,1:T(8,128)S(1)}, f32[1024,640]{0,1:T(8,128)}, u32[]{:S(2)}) copy-start(f32[1024,640]{0,1:T(8,128)} %copy-done.3) | copy-start | bytes 7864324
  (6 other events, 9.9 us)
where the time goes:
time: 103 us; the launch traced here: 102 us
  starting transfers between devices  46 us (45%)
  other arithmetic  20.7 us (20%)
  matrix products  17.7 us (17%)
  local copies, waits for them, and re-layouts  14.8 us (14%)
  waiting for transfers between devices  1.93 us (2%)
  between operations  1.31 us (1%)
    ppermute x8, starting transfers between devices, padded(): lax.ppermute(tail, axis, [(i, (i + 1) % count) for i in range(ends)])  32.2 us
    ppermute x8, starting transfers between devices, padded(): lax.ppermute(head, axis, [((i + 1) % count, i) for i in range(ends)])  13.8 us
    concatenate x6, other arithmetic, padded(): jnp.concatenate([lax.ppermute(tail, axis, [(i, (i + 1) % count) for i in...  9.29 us
    dot_general x1, matrix products, local(): jnp.einsum('nkc,kch->nh', stacked, ctx_masked, preferred_element_type=jnp...  5.8 us
    another operation x4, local copies, waits for them, and re-layouts, local(): jnp.stack([ypad[0:rows, 1:-1], ypad[2:, 1:-1], ypad[1:-1, 0:cols], ypad[1...  4.73 us
    add x2, local copies, waits for them, and re-layouts, local(): local_pre.reshape(zrows, 4, zcols, 4, hidden_units)  2.66 us
    reduce_sum x1, other arithmetic, local(): g_pre.astype(jnp.float32).reshape(zrows, 4, zcols, 4, hidden_units)  2.56 us
    dot_general x1, matrix products, local(): jnp.dot(flat, chan_masked, preferred_element_type=jnp.float32)  2.52 us
  transfers between devices with their start and end apart: 16, of which 3 were waited for; matrix products, arithmetic and copies ran while one was open for 15% of the time, Pallas kernels for 0%

commit v1 on v0

v1 whole, which is shorter than its diff:
```python
import jax
import jax.numpy as jnp
import numpy as np
from jax import lax
from jax.experimental import pallas as pl
from jax.experimental.pallas import tpu as pltpu
from jax.sharding import PartitionSpec as P

BF = jnp.bfloat16
F32 = jnp.float32
DIRS = ((-1, 0), (1, 0), (0, -1), (0, 1), (-1, -1), (-1, 1), (1, -1), (1, 1))
OPP = (1, 0, 3, 2, 7, 6, 5, 4)


def dot(a, b):
    return jnp.dot(a, b, preferred_element_type=F32)


def dot_t(a, b):
    return lax.dot_general(a, b, (((1,), (1,)), ((), ())), preferred_element_type=F32)


def tables(rows, cols, zrows, zcols, tr):
    half = cols // 2
    sub = 8
    m = np.arange(sub * half)
    ir, k = m // half, m % half
    ps = np.zeros((3 * sub * half, sub * cols), np.float32)
    n = sub * half
    ps[m, ir * cols + 2 * k + ir % 2] = 1
    ps[n + m, ir * cols + 2 * k + 1 - ir % 2] = 1
    for q in m:
        kk = k[q] + (1 if ir[q] % 2 == 0 else -1)
        if 0 <= kk < half:
            ps[2 * n + q, ir[q] * cols + 2 * kk + ir[q] % 2] = 1
    pt = ps[: 2 * n].T.copy()
    m = np.arange(tr * half)
    ir, k = m // half, m % half
    sb = np.zeros((tr * half, tr * half), np.float32)
    for q in m:
        kk = k[q] + (-1 if ir[q] % 2 == 0 else 1)
        if 0 <= kk < half:
            sb[q, ir[q] * half + kk] = 1
    m = np.arange(rows * half)
    i, k = m // half, m % half
    up = np.zeros((rows * half, zrows * zcols), np.float32)
    up[m, (i // 4) * zcols + k // 2] = 1
    qf = np.zeros((rows * half, rows), np.float32)
    qb = np.zeros((rows * half, rows), np.float32)
    ef = np.zeros((rows, rows * half), np.float32)
    eb = np.zeros((rows, rows * half), np.float32)
    for r in range(rows):
        e = r // 2 + (rows // 2 if r % 2 else 0)
        qf[r * half + (half - 1 if r % 2 == 0 else 0), e] = 1
        qb[r * half + (0 if r % 2 == 0 else half - 1), e] = 1
        ef[e, r * half + (0 if r % 2 == 0 else half - 1)] = 1
        eb[e, r * half + (half - 1 if r % 2 == 0 else 0)] = 1
    cells = zrows * zcols
    tz = np.zeros((9 * cells, cells + 8 * 16), np.float32)
    for a in range(3):
        for b in range(3):
            for zi in range(zrows):
                for zj in range(zcols):
                    y, x = zi + a - 1, zj + b - 1
                    dr = -1 if y < 0 else (1 if y >= zrows else 0)
                    dc = -1 if x < 0 else (1 if x >= zcols else 0)
                    if (dr, dc) == (0, 0):
                        s = y * zcols + x
                    else:
                        s = cells + 16 * DIRS.index((dr, dc))
                        if dr == 0:
                            s += y
                        else:
                            s += (16 - zcols if dr < 0 else 0) + x % zcols
                    tz[(a * 3 + b) * cells + zi * zcols + zj, s] = 1
    ez = np.zeros((32, cells), np.float32)
    for zi in range(zrows):
        ez[zi, zi * zcols] = 1
        ez[16 + zi, zi * zcols + zcols - 1] = 1
    m = np.arange(tr * half)
    ir, k = m // half, m % half
    w = tr * half
    rg = np.zeros((tr, 2 * w), np.float32)
    rg[ir, m] = 1
    rg[ir, w + m] = 1
    cm = np.zeros((2 * w, cols), np.float32)
    cm[m, 2 * k + ir % 2] = 1
    cm[w + m, 2 * k + 1 - ir % 2] = 1
    return [x.astype(jnp.bfloat16) for x in (ps, pt, sb, up, up.T.copy(), qf, qb, ef, eb, tz, ez, rg, cm)]


def make_kernel(rows, cols, ch, zrows, zcols, zch, hid, tr, nrow, ncol):
    half = cols // 2
    full = (ch // 256) * 256
    rem = ch - full
    cp = full + 2 * rem
    cells = zrows * zcols
    w = tr * half
    tiles = rows // tr
    own = rows * half

    def kernel(*refs):
        (bounds, latent, hyper, hw_in, pw_in, cw_in, kw_in, ow_in, *tabs) = refs[:21]
        rate_out, gl_out, gh_out = refs[21:24]
        (lat, hw, wt, owr, wo, ps, pt, sb, up, upt, qf, qb, ef, eb, tz, ez, rg, cm,
         ae, nn, ss, hcf, csf, he, csh, gne, ga, rs, hcb, csb, gz, csz, in_sem, send_sem, recv_sem) = refs[24:]
        tab_v = (ps, pt, sb, up, upt, qf, qb, ef, eb, tz, ez, rg, cm)
        my_r = lax.axis_index("row")
        my_c = lax.axis_index("col")

        def there(d):
            dr, dc = DIRS[d]
            ok = my_r >= 0
            if dr < 0:
                ok = my_r > 0
            if dr > 0:
                ok = my_r < nrow - 1
            if dc < 0:
                ok = ok & (my_c > 0)
            if dc > 0:
                ok = ok & (my_c < ncol - 1)
            return ok

        def dev(d):
            return {"row": my_r + DIRS[d][0], "col": my_c + DIRS[d][1]}

        barrier = pltpu.get_barrier_semaphore()
        for d in range(8):
            @pl.when(there(d))
            def _(d=d):
                pl.semaphore_signal(barrier, inc=1, device_id=dev(d), device_id_type=pl.DeviceIdType.MESH)

        loads = []

        def load(src, dst):
            c = pltpu.make_async_copy(src, dst, in_sem.at[len(loads)])
            c.start()
            loads.append(c)
            return len(loads) - 1

        ld_lat = load(latent, lat)
        ld_hyper = load(hyper, he.at[pl.ds(0, cells)])
        ld_tab = [load(a, b) for a, b in zip(tabs, tab_v)]
        ld_hw = load(hw_in, hw)
        ld_w = []
        for d in range(4):
            ld_w.append(load(cw_in.at[pl.ds(d * ch, full)], wt.at[pl.ds(d * full, full)]))
            ld_w.append(load(cw_in.at[pl.ds(d * ch + full, rem)], wt.at[pl.ds(5 * full + d * rem, rem)]))
        ld_w.append(load(kw_in.at[pl.ds(0, full)], wt.at[pl.ds(4 * full, full)]))
        ld_w.append(load(kw_in.at[pl.ds(full, rem)], wt.at[pl.ds(5 * full + 4 * rem, rem)]))
        ld_w.append(load(pw_in.at[pl.ds(128, zch - 128)], wt.at[pl.ds(5 * ch, zch - 128)]))
        ld_w.append(load(pw_in.at[pl.ds(0, 128)], wt.at[pl.ds(5 * ch + zch - 128, 128)]))
        ld_ow = load(ow_in, owr)

        def absent(d, fill):
            @pl.when(jnp.logical_not(there(d)))
            def _():
                fill()

        def zero(ref, start, size):
            def fill():
                ref[pl.ds(start, size), :] = jnp.zeros((size, ref.shape[1]), ref.dtype)
            return fill

        for d in range(8):
            absent(d, zero(he, cells + 16 * d, 16))
            absent(d, zero(gz, cells + 16 * d, 16))
        absent(0, zero(ae, 0, half))
        absent(1, zero(ae, half + own, half))
        absent(0, zero(gne, 0, half))
        absent(1, zero(gne, half + own, half))
        hr = rows // 2
        absent(3, zero(hcf, 0, hr))
        absent(2, zero(hcf, hr, hr))
        absent(2, zero(hcb, 0, hr))
        absent(3, zero(hcb, hr, hr))

        def remote(idx, d, src, dst):
            return pltpu.make_async_remote_copy(
                src_ref=src, dst_ref=dst, send_sem=send_sem.at[idx], recv_sem=recv_sem.at[idx],
                device_id=dev(d), device_id_type=pl.DeviceIdType.MESH)

        def hyper_copies(base, ext, col):
            out = []
            for d, (dr, dc) in enumerate(DIRS):
                if dr < 0:
                    src = ext.at[pl.ds(0, 16)]
                elif dr > 0:
                    src = ext.at[pl.ds(cells - 16, 16)]
                else:
                    src = col.at[pl.ds(0 if dc < 0 else 16, 16)]
                out.append((d, OPP[d], remote(base + OPP[d], d, src, ext.at[pl.ds(cells + 16 * OPP[d], 16)])))
            return out

        def side_copies(base, ext, col, halo, left_first):
            lf = 0 if left_first else hr
            rf = hr - lf
            return [
                (0, 1, remote(base + 1, 0, ext.at[pl.ds(half, half)], ext.at[pl.ds(half + own, half)])),
                (1, 0, remote(base + 0, 1, ext.at[pl.ds(own, half)], ext.at[pl.ds(0, half)])),
                (2, 3, remote(base + 3, 2, col.at[pl.ds(lf, hr)], halo.at[pl.ds(lf, hr)])),
                (3, 2, remote(base + 2, 3, col.at[pl.ds(rf, hr)], halo.at[pl.ds(rf, hr)])),
            ]

        hyper_c = hyper_copies(0, he, csh)
        lat_c = side_copies(8, ae, csf, hcf, True)
        gpre_c = side_copies(12, gne, csb, hcb, False)
        gz_c = hyper_copies(16, gz, csz)

        def start(copies):
            for d, _, c in copies:
                @pl.when(there(d))
                def _(c=c):
                    c.start()

        def wait_recv(copies):
            for _, o, c in copies:
                @pl.when(there(o))
                def _(c=c):
                    c.wait_recv()

        def wait_send(copies):
            for d, _, c in copies:
                @pl.when(there(d))
                def _(c=c):
                    c.wait_send()

        loads[ld_lat].wait()
        loads[ld_hyper].wait()
        for i in ld_tab:
            loads[i].wait()
        csh[...] = dot(ez[...], he[pl.ds(0, cells), :]).astype(BF)
        n8 = 8 * half
        for t in range(rows // 8):
            y = dot(ps[...], lat[pl.ds(t * 8 * cols, 8 * cols), :])
            y = jnp.concatenate([y[:, :full], y[:, full:], y[:, full:]], axis=1).astype(BF)
            ae[pl.ds(half + t * n8, n8), :] = y[:n8]
            nn[pl.ds(t * n8, n8), :] = y[n8 : 2 * n8]
            ss[pl.ds(t * n8, n8), :] = y[2 * n8 :]
        csf[...] = dot(ef[...], ae[pl.ds(half, own), :]).astype(BF)

        count = jnp.int32(0)
        for d in range(8):
            count = count + there(d).astype(jnp.int32)
        pl.semaphore_wait(barrier, count)
        start(hyper_c)
        start(lat_c)

        def ids(shape, dim, period, width):
            c = lax.broadcasted_iota(jnp.int32, shape, dim)
            c = jnp.where(c >= period, c - period, c)
            s = jnp.zeros(shape, jnp.int32)
            for g in range(1, 5):
                s = s + (c >= bounds[g]).astype(jnp.int32)
            return jnp.where(c < width, s, -1)

        col_id = ids((1, hid), 1, ch, ch)
        row_id = ids((ch, 1), 0, ch, ch)
        same = jnp.where(row_id == col_id, 1.0, 0.0).astype(BF)
        prev = jnp.where(row_id < col_id, 1.0, 0.0).astype(BF)
        for i in ld_w:
            loads[i].wait()
        for d in range(5):
            mask = prev if d == 4 else same
            a = pl.ds(d * full, full)
            wt[a, :] = wt[a, :] * mask[:full]
            b = pl.ds(5 * full + d * rem, rem)
            wt[b, :] = wt[b, :] * mask[full:]
        hid_id = ids((hid, 1), 0, ch, ch)
        par_id = ids((1, 2 * cp), 1, cp, ch)
        omask = jnp.where(hid_id == par_id, 1.0, 0.0).astype(BF)
        loads[ld_ow].wait()
        raw = owr[...].astype(F32)
        pad = jnp.zeros((hid, cp - ch), F32)
        wide = jnp.concatenate([raw[:, :ch], pad, raw[:, ch:], pad], axis=1).astype(BF)
        wo[...] = wide * omask

        loads[ld_hw].wait()
        wait_recv(hyper_c)
        taps = dot(tz[...], he[...]).astype(BF)
        hz = jnp.zeros((cells, zch), F32)
        for ab in range(9):
            hz = hz + dot(taps[ab * cells : (ab + 1) * cells], hw[pl.ds(ab * zch, zch), :])
        sz = jax.nn.sigmoid(hz)
        dz = sz * (1.0 + hz * (1.0 - sz))
        f = hz * sz
        feat = jnp.concatenate([jnp.zeros((cells, rem), F32), f[:, 128:], f[:, :128]], axis=1).astype(BF)
        wait_recv(lat_c)

        def mix(even, odd):
            return jnp.concatenate(
                [(even if i % 2 == 0 else odd)[i * half : (i + 1) * half] for i in range(tr)], axis=0)

        lane = lax.broadcasted_iota(jnp.int32, (w, 2 * rem), 1)
        left = lane < rem

        def pair(a, b):
            return jnp.where(left, a, b)

        kidx = lax.broadcasted_iota(jnp.int32, (2 * w, cp), 1)
        gsum = jnp.zeros((cells, hid), F32)
        for t in range(tiles):
            at = t * w
            a = ae[pl.ds(half + at, w), :]
            au = ae[pl.ds(at, w), :]
            ad = ae[pl.ds(2 * half + at, w), :]
            o = nn[pl.ds(at, w), :]
            s = (ss[pl.ds(at, w), :].astype(F32) + dot(qf[pl.ds(at, w), :], hcf[...])).astype(BF)
            al = mix(a, s)
            ar = mix(s, a)
            hup = dot(up[pl.ds(at, w), :], feat).astype(BF)
            h0, h1 = hup[:, : 2 * rem], hup[:, 2 * rem :]
            x = jnp.concatenate(
                [au[:, :full], ad[:, :full], al[:, :full], ar[:, :full], o[:, :full],
                 pair(au[:, full:], ad[:, full:]), pair(al[:, full:], ar[:, full:]),
                 pair(o[:, full:], h0), h1], axis=1)
            pre_n = dot(x, wt[...])
            xa = jnp.concatenate([pair(a[:, full:], h0), h1], axis=1)
            pre_a = dot(a[:, :full], wt[pl.ds(4 * full, full), :]) + dot(
                xa, wt[pl.ds(5 * full + 4 * rem, rem + zch), :])
            pre = jnp.concatenate([pre_a, pre_n], axis=0)
            sg = 0.5 * jnp.tanh(0.5 * pre) + 0.5
            hidden = pre * sg
            ds = sg + hidden * (1.0 - sg)
            par = dot(hidden.astype(BF), wo[...])
            mu = par[:, :cp]
            sraw = par[:, cp:]
            e = jnp.exp(-jnp.abs(sraw))
            sigma = 0.11 + (jnp.maximum(sraw, 0.0) + jnp.log(1.0 + e))
            inv = 1.0 / sigma
            y = jnp.concatenate([a, o], axis=0).astype(F32)
            r = (y - mu) * inv
            nll = 0.5 * r * r + jnp.log(sigma)
            rate = jnp.sum(jnp.where(kidx < ch, nll, 0.0), axis=1, keepdims=True) * (1.0 / ch)
            spread = rate * cm[...].astype(F32)
            hi = spread.astype(BF)
            lo = (spread - hi.astype(F32)).astype(BF)
            rate_out[pl.ds(t * tr, tr), :] = dot(rg[...], hi) + dot(rg[...], lo)
            rsig = r * inv
            rs[pl.ds(2 * at, 2 * w), :] = rsig
            sgs = jnp.where(sraw >= 0.0, 1.0, e) / (1.0 + e)
            g_par = jnp.concatenate([-rsig, (1.0 - r * r) * inv * sgs], axis=1).astype(BF)
            gp = (dot_t(g_par, wo[...]) * ds).astype(BF)
            ga[pl.ds(at, w), :] = gp[:w]
            gne[pl.ds(half + at, w), :] = gp[w:]
            ut = upt[:, at : at + w]
            gsum = gsum + dot(ut, gp[:w]) + dot(ut, gp[w:])

        csb[...] = dot(eb[...], gne[pl.ds(half, own), :]).astype(BF)
        start(gpre_c)

        hi = gsum.astype(BF)
        lo = (gsum - hi.astype(F32)).astype(BF)
        both = jnp.concatenate([hi, lo], axis=0)
        p0 = dot_t(both, wt[pl.ds(5 * ch + zch - 128, 128), :])
        p1 = dot_t(both, wt[pl.ds(5 * ch, zch - 128), :])
        g_h = jnp.concatenate([p0[:cells] + p0[cells:], p1[:cells] + p1[cells:]], axis=1)
        g_hz = (g_h * dz).astype(BF)
        gz[pl.ds(0, cells), :] = g_hz
        csz[...] = dot(ez[...], g_hz).astype(BF)
        start(gz_c)

        wait_recv(gpre_c)
        wcm = wt[pl.ds(4 * full, full), :]
        wcr = wt[pl.ds(5 * full + 4 * rem, rem), :]
        for t in range(tiles):
            at = t * w
            gn = gne[pl.ds(half + at, w), :]
            gu = gne[pl.ds(at, w), :]
            gd = gne[pl.ds(2 * half + at, w), :]
            s = (dot(sb[...], gn) + dot(qb[pl.ds(at, w), :], hcb[...])).astype(BF)
            gr = mix(gn, s)
            gl = mix(s, gn)
            gs = (gd, gu, gr, gl, ga[pl.ds(at, w), :])
            m = rs[pl.ds(2 * at, w), :full]
            q = rs[pl.ds(2 * at, w), full:ch]
            for d in range(5):
                m = m + dot_t(gs[d], wt[pl.ds(d * full, full), :])
                q = q + dot_t(gs[d], wt[pl.ds(5 * full + d * rem, rem), :])
            nm = rs[pl.ds(2 * at + w, w), :full] + dot_t(gn, wcm)
            nq = rs[pl.ds(2 * at + w, w), full:ch] + dot_t(gn, wcr)
            va = jnp.concatenate([m, q], axis=1).astype(BF)
            vn = jnp.concatenate([nm, nq], axis=1).astype(BF)
            for u in range(tr // 8):
                v = jnp.concatenate([va[u * n8 : (u + 1) * n8], vn[u * n8 : (u + 1) * n8]], axis=0)
                gl_out[pl.ds((t * tr + u * 8) * cols, 8 * cols), :] = dot(pt[...], v).astype(BF)

        wait_recv(gz_c)
        taps = dot(tz[...], gz[...]).astype(BF)
        acc = jnp.zeros((cells, zch), F32)
        for ab in range(9):
            back = 8 - ab
            acc = acc + dot_t(taps[back * cells : (back + 1) * cells], hw[pl.ds(ab * zch, zch), :])
        gh_out[...] = acc

        wait_send(hyper_c)
        wait_send(lat_c)
        wait_send(gpre_c)
        wait_send(gz_c)

    return kernel


def solution(mesh):
    nrow, ncol = mesh.shape["row"], mesh.shape["col"]

    def local(latent, hyper, bounds, hyper_weight, prior_weight, ctx_weight, chan_weight, out_weight):
        rows, cols, ch = latent.shape
        zrows, zcols, zch = hyper.shape
        hid = prior_weight.shape[1]
        tr = 16
        half = cols // 2
        full = (ch // 256) * 256
        rem = ch - full
        cp = full + 2 * rem
        cells = zrows * zcols
        own = rows * half
        tabs = tables(rows, cols, zrows, zcols, tr)
        hr = rows // 2
        anyspec = pl.BlockSpec(memory_space=pl.ANY)
        vm = pl.BlockSpec(memory_space=pltpu.VMEM)
        v = lambda *s, dt=BF: pltpu.VMEM(s, dt)
        scratch = [
            v(rows * cols, ch), v(9 * zch, zch), v(5 * ch + zch, hid), v(hid, hid), v(hid, 2 * cp),
            *[v(*t.shape) for t in tabs],
            v(own + 2 * half, cp), v(own, cp), v(own, cp), v(2 * hr, cp), v(2 * hr, cp),
            v(cells + 128, zch), v(32, zch),
            v(own + 2 * half, hid), v(own, hid), v(rows * cols, cp, dt=F32), v(2 * hr, hid), v(2 * hr, hid),
            v(cells + 128, zch), v(32, zch),
            pltpu.SemaphoreType.DMA((32,)), pltpu.SemaphoreType.DMA((24,)), pltpu.SemaphoreType.DMA((24,)),
        ]
        rate, gl, gh = pl.pallas_call(
            make_kernel(rows, cols, ch, zrows, zcols, zch, hid, tr, nrow, ncol),
            out_shape=(
                jax.ShapeDtypeStruct((rows, cols), F32),
                jax.ShapeDtypeStruct((rows * cols, ch), BF),
                jax.ShapeDtypeStruct((cells, zch), F32),
            ),
            in_specs=[pl.BlockSpec(memory_space=pltpu.SMEM)] + [anyspec] * (7 + len(tabs)),
            out_specs=(vm, vm, vm),
            scratch_shapes=scratch,
            compiler_params=pltpu.CompilerParams(
                collective_id=0, has_side_effects=True, vmem_limit_bytes=56 * 1024 * 1024),
        )(
            bounds, latent.reshape(rows * cols, ch), hyper.reshape(cells, zch),
            hyper_weight.reshape(9 * zch, zch), prior_weight, ctx_weight.reshape(4 * ch, hid),
            chan_weight, out_weight, *[jnp.asarray(t) for t in tabs],
        )
        return rate, gl.reshape(rows, cols, ch), gh.reshape(zrows, zcols, zch)

    in_specs = (
        P(("parts", "row"), "col", None),
        P(("parts", "row"), "col", None),
        P(),
        P(),
        P(),
        P(),
        P(),
        P(),
    )
    out_specs = (
        P(("parts", "row"), "col"),
        P(("parts", "row"), "col", None),
        P(("parts", "row"), "col", None),
    )
    return jax.shard_map(local, mesh=mesh, in_specs=in_specs, out_specs=out_specs, check_vma=False)
```

time: 103 us -> 29.9 us (0.29)
  the two profiles are of different devices: /device:TPU:1 before, /device:TPU:0 now
where the time goes in v1:
time: 29.9 us; the launch traced here: 29.6 us
  Pallas kernels  24.9 us (83%)
  local copies, waits for them, and re-layouts  4.08 us (14%)
  between operations  0.65 us (2%)
    pallas_call x1, Pallas kernels, local(): pl.pallas_call(make_kernel(rows, cols, ch, zrows, zcols, zch, hid, tr, nr...  24.9 us
    unnamed x5, local copies, waits for them, and re-layouts  4.08 us

profile of v1, /device:TPU:0, one launch (start us, length us, event | category | flops | bytes accessed | tf_op | source)
XLA Modules:
  0.0 29.6 jit_solution(7605286113262632201)
XLA Ops:
  0.6 24.9 %shard_map.220 = (f32[32,32]{1,0:T(8,128)}, bf16[1024,320]{1,0:T(8,128)(2,1)}, f32[64,192]{1,0:T(8,128)}) custom-call(s32[6]{0:T(128)} %refs_0_.1, bf16[1024,320]{1,0:T(8,128)(2,1)} %bitcast.8, bf16[64,192]{1,0:T(8,128)(2,1)} %bitcast.11, bf16[1728,192]{1,0:T(8,128)(2,1)} %bitcast.7, bf16[192,640]{1,0:T(8,128)(2,1)} %refs_4_.1, bf16[1280,640]{1,0:T(8,128)(2,1)} %bitcast.6, ...), custom_call_target="tpu_custom_call" | custom-call | tf_op jit(solution)/shard_map/pallas_call | solution.py:432
  25.5 0.0 copy-start
  25.5 1.4 %copy.27 = f32[32,32]{1,0:T(8,128)} copy(f32[32,32]{1,0:T(8,128)} %get-tuple-element.12) | data formatting | bytes 8192
  26.9 2.1 %copy.28 = bf16[32,32,320]{2,1,0:T(8,128)(2,1)} copy(bf16[32,32,320]{2,1,0:T(8,128)(2,1)} %bitcast.9) | data formatting | bytes 1310720
  29.0 0.0 copy-done
  29.0 0.6 %copy.29 = f32[8,8,192]{2,1,0:T(8,128)} copy(f32[8,8,192]{2,1,0:T(8,128)S(1)} %bitcast.10) | data formatting | bytes 98304
Async XLA Ops:
  25.5 3.5 %copy-start = (f32[64,192]{1,0:T(8,128)S(1)}, f32[64,192]{1,0:T(8,128)}, u32[]{:S(2)}) copy-start(f32[64,192]{1,0:T(8,128)} %get-tuple-element.8) | copy-start | bytes 147460

commit v2 on v1

--- a/solution.py
+++ b/solution.py
@@ -103,7 +103,8 @@
         (bounds, latent, hyper, hw_in, pw_in, cw_in, kw_in, ow_in, *tabs) = refs[:21]
         rate_out, gl_out, gh_out = refs[21:24]
         (lat, hw, wt, owr, wo, ps, pt, sb, up, upt, qf, qb, ef, eb, tz, ez, rg, cm,
-         ae, nn, ss, hcf, csf, he, csh, gne, ga, rs, hcb, csb, gz, csz, in_sem, send_sem, recv_sem) = refs[24:]
+         ae, nn, ss, hcf, csf, he, csh, gne, ga, rs, hcb, csb, gz, csz, rate_v, gl_v, gh_v,
+         in_sem, out_sem, send_sem, recv_sem) = refs[24:]
         tab_v = (ps, pt, sb, up, upt, qf, qb, ef, eb, tz, ez, rg, cm)
         my_r = lax.axis_index("row")
         my_c = lax.axis_index("col")
@@ -140,8 +141,8 @@
 
         ld_lat = load(latent, lat)
         ld_hyper = load(hyper, he.at[pl.ds(0, cells)])
-        ld_tab = [load(a, b) for a, b in zip(tabs, tab_v)]
-        ld_hw = load(hw_in, hw)
+        early = (0, 7, 10)
+        ld_early = [load(tabs[i], tab_v[i]) for i in early]
         ld_w = []
         for d in range(4):
             ld_w.append(load(cw_in.at[pl.ds(d * ch, full)], wt.at[pl.ds(d * full, full)]))
@@ -151,6 +152,8 @@
         ld_w.append(load(pw_in.at[pl.ds(128, zch - 128)], wt.at[pl.ds(5 * ch, zch - 128)]))
         ld_w.append(load(pw_in.at[pl.ds(0, 128)], wt.at[pl.ds(5 * ch + zch - 128, 128)]))
         ld_ow = load(ow_in, owr)
+        ld_hw = load(hw_in, hw)
+        ld_late = [load(tabs[i], tab_v[i]) for i in range(len(tabs)) if i not in early]
 
         def absent(d, fill):
             @pl.when(jnp.logical_not(there(d)))
@@ -227,7 +230,7 @@
 
         loads[ld_lat].wait()
         loads[ld_hyper].wait()
-        for i in ld_tab:
+        for i in ld_early:
             loads[i].wait()
         csh[...] = dot(ez[...], he[pl.ds(0, cells), :]).astype(BF)
         n8 = 8 * half
@@ -276,6 +279,8 @@
         wo[...] = wide * omask
 
         loads[ld_hw].wait()
+        for i in ld_late:
+            loads[i].wait()
         wait_recv(hyper_c)
         taps = dot(tz[...], he[...]).astype(BF)
         hz = jnp.zeros((cells, zch), F32)
@@ -298,8 +303,8 @@
             return jnp.where(left, a, b)
 
         kidx = lax.broadcasted_iota(jnp.int32, (2 * w, cp), 1)
-        gsum = jnp.zeros((cells, hid), F32)
-        for t in range(tiles):
+
+        def stage_pre(t):
             at = t * w
             a = ae[pl.ds(half + at, w), :]
             au = ae[pl.ds(at, w), :]
@@ -318,33 +323,58 @@
             xa = jnp.concatenate([pair(a[:, full:], h0), h1], axis=1)
             pre_a = dot(a[:, :full], wt[pl.ds(4 * full, full), :]) + dot(
                 xa, wt[pl.ds(5 * full + 4 * rem, rem + zch), :])
-            pre = jnp.concatenate([pre_a, pre_n], axis=0)
+            return jnp.concatenate([pre_a, pre_n], axis=0)
+
+        def stage_hidden(pre):
             sg = 0.5 * jnp.tanh(0.5 * pre) + 0.5
             hidden = pre * sg
-            ds = sg + hidden * (1.0 - sg)
-            par = dot(hidden.astype(BF), wo[...])
+            return hidden.astype(BF), sg + hidden * (1.0 - sg)
+
+        def stage_nll(t, par):
+            at = t * w
             mu = par[:, :cp]
             sraw = par[:, cp:]
             e = jnp.exp(-jnp.abs(sraw))
-            sigma = 0.11 + (jnp.maximum(sraw, 0.0) + jnp.log(1.0 + e))
+            e1 = 1.0 + e
+            sigma = 0.11 + (jnp.maximum(sraw, 0.0) + jnp.log(e1))
             inv = 1.0 / sigma
-            y = jnp.concatenate([a, o], axis=0).astype(F32)
+            y = jnp.concatenate([ae[pl.ds(half + at, w), :], nn[pl.ds(at, w), :]], axis=0).astype(F32)
             r = (y - mu) * inv
             nll = 0.5 * r * r + jnp.log(sigma)
+            rsig = r * inv
+            rs[pl.ds(2 * at, 2 * w), :] = rsig
+            sgs = jnp.where(sraw >= 0.0, 1.0, e) / e1
+            g_par = jnp.concatenate([-rsig, (1.0 - r * r) * inv * sgs], axis=1).astype(BF)
+            return nll, g_par
+
+        def stage_rate(t, nll):
             rate = jnp.sum(jnp.where(kidx < ch, nll, 0.0), axis=1, keepdims=True) * (1.0 / ch)
             spread = rate * cm[...].astype(F32)
             hi = spread.astype(BF)
             lo = (spread - hi.astype(F32)).astype(BF)
-            rate_out[pl.ds(t * tr, tr), :] = dot(rg[...], hi) + dot(rg[...], lo)
-            rsig = r * inv
-            rs[pl.ds(2 * at, 2 * w), :] = rsig
-            sgs = jnp.where(sraw >= 0.0, 1.0, e) / (1.0 + e)
-            g_par = jnp.concatenate([-rsig, (1.0 - r * r) * inv * sgs], axis=1).astype(BF)
-            gp = (dot_t(g_par, wo[...]) * ds).astype(BF)
+            rate_v[pl.ds(t * tr, tr), :] = dot(rg[...], hi) + dot(rg[...], lo)
+
+        def stage_gp(t, g_hid, ds):
+            at = t * w
+            gp = (g_hid * ds).astype(BF)
             ga[pl.ds(at, w), :] = gp[:w]
             gne[pl.ds(half + at, w), :] = gp[w:]
             ut = upt[:, at : at + w]
-            gsum = gsum + dot(ut, gp[:w]) + dot(ut, gp[w:])
+            return dot(ut, gp[:w]) + dot(ut, gp[w:])
+
+        every = range(tiles)
+        pres, hids, pars, nlls, hback, gsums = [], [], [], [], [], []
+        for t in every:
+            pres.append(stage_pre(t))
+        for t in every:
+            hids.append(stage_hidden(pres[t]))
+            pars.append(dot(hids[t][0], wo[...]))
+        for t in every:
+            nlls.append(stage_nll(t, pars[t]))
+            hback.append(dot_t(nlls[t][1], wo[...]))
+        for t in every:
+            gsums.append(stage_gp(t, hback[t], hids[t][1]))
+        gsum = sum(gsums[1:], gsums[0])
 
         csb[...] = dot(eb[...], gne[pl.ds(half, own), :]).astype(BF)
         start(gpre_c)
@@ -360,30 +390,52 @@
         csz[...] = dot(ez[...], g_hz).astype(BF)
         start(gz_c)
 
+        def main_w(d):
+            return wt[pl.ds(d * full, full), :]
+
+        def rest_w(d):
+            return wt[pl.ds(5 * full + d * rem, rem), :]
+
+        shifts, vns = [], []
+        for t in every:
+            at = t * w
+            gn = gne[pl.ds(half + at, w), :]
+            shifts.append(dot(sb[...], gn))
+            nm = rs[pl.ds(2 * at + w, w), :full] + dot_t(gn, main_w(4))
+            nq = rs[pl.ds(2 * at + w, w), full:ch] + dot_t(gn, rest_w(4))
+            vns.append(jnp.concatenate([nm, nq], axis=1).astype(BF))
+            gs = ga[pl.ds(at, w), :]
+            m = rs[pl.ds(2 * at, w), :full] + dot_t(gs, main_w(4))
+            q = rs[pl.ds(2 * at, w), full:ch] + dot_t(gs, rest_w(4))
+            rs[pl.ds(2 * at, w), :full] = m
+            rs[pl.ds(2 * at, w), full:ch] = q
+            stage_rate(t, nlls[t][0])
+        rate_copy = pltpu.make_async_copy(rate_v, rate_out, out_sem.at[0])
+        rate_copy.start()
+
         wait_recv(gpre_c)
-        wcm = wt[pl.ds(4 * full, full), :]
-        wcr = wt[pl.ds(5 * full + 4 * rem, rem), :]
-        for t in range(tiles):
+        outs = [rate_copy]
+        for t in every:
             at = t * w
             gn = gne[pl.ds(half + at, w), :]
             gu = gne[pl.ds(at, w), :]
             gd = gne[pl.ds(2 * half + at, w), :]
-            s = (dot(sb[...], gn) + dot(qb[pl.ds(at, w), :], hcb[...])).astype(BF)
-            gr = mix(gn, s)
-            gl = mix(s, gn)
-            gs = (gd, gu, gr, gl, ga[pl.ds(at, w), :])
+            s = (shifts[t] + dot(qb[pl.ds(at, w), :], hcb[...])).astype(BF)
+            gs = (gd, gu, mix(gn, s), mix(s, gn))
             m = rs[pl.ds(2 * at, w), :full]
             q = rs[pl.ds(2 * at, w), full:ch]
-            for d in range(5):
-                m = m + dot_t(gs[d], wt[pl.ds(d * full, full), :])
-                q = q + dot_t(gs[d], wt[pl.ds(5 * full + d * rem, rem), :])
-            nm = rs[pl.ds(2 * at + w, w), :full] + dot_t(gn, wcm)
-            nq = rs[pl.ds(2 * at + w, w), full:ch] + dot_t(gn, wcr)
+            for d in range(4):
+                m = m + dot_t(gs[d], main_w(d))
+                q = q + dot_t(gs[d], rest_w(d))
             va = jnp.concatenate([m, q], axis=1).astype(BF)
-            vn = jnp.concatenate([nm, nq], axis=1).astype(BF)
+            vn = vns[t]
             for u in range(tr // 8):
                 v = jnp.concatenate([va[u * n8 : (u + 1) * n8], vn[u * n8 : (u + 1) * n8]], axis=0)
-                gl_out[pl.ds((t * tr + u * 8) * cols, 8 * cols), :] = dot(pt[...], v).astype(BF)
+                gl_v[pl.ds((t * tr + u * 8) * cols, 8 * cols), :] = dot(pt[...], v).astype(BF)
+            span = pl.ds(t * tr * cols, tr * cols)
+            c = pltpu.make_async_copy(gl_v.at[span], gl_out.at[span], out_sem.at[2 + t])
+            c.start()
+            outs.append(c)
 
         wait_recv(gz_c)
         taps = dot(tz[...], gz[...]).astype(BF)
@@ -391,7 +443,12 @@
         for ab in range(9):
             back = 8 - ab
             acc = acc + dot_t(taps[back * cells : (back + 1) * cells], hw[pl.ds(ab * zch, zch), :])
-        gh_out[...] = acc
+        gh_v[...] = acc
+        c = pltpu.make_async_copy(gh_v, gh_out, out_sem.at[1])
+        c.start()
+        outs.append(c)
+        for c in outs:
+            c.wait()
 
         wait_send(hyper_c)
         wait_send(lat_c)
@@ -399,6 +456,30 @@
         wait_send(gz_c)
 
     return kernel
+
+
+def move(rate, gl, gh, rate_out, gl_out, gh_out, sem):
+    parts = 4
+    size = gl.shape[0] // parts
+    copies = [pltpu.make_async_copy(rate, rate_out, sem.at[0]), pltpu.make_async_copy(gh, gh_out, sem.at[1])]
+    for i in range(parts):
+        span = pl.ds(i * size, size)
+        copies.append(pltpu.make_async_copy(gl.at[span], gl_out.at[span], sem.at[2 + i]))
+    for c in copies:
+        c.start()
+    for c in copies:
+        c.wait()
+
+
+def finish(*arrays):
+    anyspec = pl.BlockSpec(memory_space=pl.ANY)
+    return pl.pallas_call(
+        move,
+        out_shape=tuple(jax.ShapeDtypeStruct(a.shape, a.dtype) for a in arrays),
+        in_specs=[anyspec] * 3,
+        out_specs=(anyspec,) * 3,
+        scratch_shapes=[pltpu.SemaphoreType.DMA((6,))],
+    )(*arrays)
 
 
 def solution(mesh):
@@ -418,7 +499,6 @@
         tabs = tables(rows, cols, zrows, zcols, tr)
         hr = rows // 2
         anyspec = pl.BlockSpec(memory_space=pl.ANY)
-        vm = pl.BlockSpec(memory_space=pltpu.VMEM)
         v = lambda *s, dt=BF: pltpu.VMEM(s, dt)
         scratch = [
             v(rows * cols, ch), v(9 * zch, zch), v(5 * ch + zch, hid), v(hid, hid), v(hid, 2 * cp),
@@ -427,7 +507,8 @@
             v(cells + 128, zch), v(32, zch),
             v(own + 2 * half, hid), v(own, hid), v(rows * cols, cp, dt=F32), v(2 * hr, hid), v(2 * hr, hid),
             v(cells + 128, zch), v(32, zch),
-            pltpu.SemaphoreType.DMA((32,)), pltpu.SemaphoreType.DMA((24,)), pltpu.SemaphoreType.DMA((24,)),
+            v(rows, cols, dt=F32), v(rows * cols, ch), v(cells, zch, dt=F32),
+            pltpu.SemaphoreType.DMA((32,)), pltpu.SemaphoreType.DMA((2 + rows // tr,)), pltpu.SemaphoreType.DMA((24,)), pltpu.SemaphoreType.DMA((24,)),
         ]
         rate, gl, gh = pl.pallas_call(
             make_kernel(rows, cols, ch, zrows, zcols, zch, hid, tr, nrow, ncol),
@@ -437,7 +518,7 @@
                 jax.ShapeDtypeStruct((cells, zch), F32),
             ),
             in_specs=[pl.BlockSpec(memory_space=pltpu.SMEM)] + [anyspec] * (7 + len(tabs)),
-            out_specs=(vm, vm, vm),
+            out_specs=(anyspec, anyspec, anyspec),
             scratch_shapes=scratch,
             compiler_params=pltpu.CompilerParams(
                 collective_id=0, has_side_effects=True, vmem_limit_bytes=56 * 1024 * 1024),
@@ -446,6 +527,7 @@
             hyper_weight.reshape(9 * zch, zch), prior_weight, ctx_weight.reshape(4 * ch, hid),
             chan_weight, out_weight, *[jnp.asarray(t) for t in tabs],
         )
+        rate, gl, gh = finish(rate, gl, gh)
         return rate, gl.reshape(rows, cols, ch), gh.reshape(zrows, zcols, zch)
 
     in_specs = (

time: 29.9 us -> 50.6 us (1.69)
  Pallas kernels: 24.9 us -> 49.8 us
  local copies, waits for them, and re-layouts: 4.08 us -> 0 us
    pallas_call x0 -> x1, Pallas kernels: none -> 27.5 us  [finish(): pl.pallas_call(move, out_shape=tuple((jax.ShapeDtypeStruct(a.shape, a.dty...]
    unnamed x5 -> x0, local copies, waits for them, and re-layouts: 4.08 us -> none
    pallas_call x1, Pallas kernels: 24.9 us -> 22.3 us  [local(): pl.pallas_call(make_kernel(rows, cols, ch, zrows, zcols, zch, hid, tr, nr...]
where the time goes in v2:
time: 50.6 us; the launch traced here: 50.4 us
  Pallas kernels  49.8 us (98%)
  between operations  0.64 us (1%)
    pallas_call x1, Pallas kernels, finish(): pl.pallas_call(move, out_shape=tuple((jax.ShapeDtypeStruct(a.shape, a.dty...  27.5 us
    pallas_call x1, Pallas kernels, local(): pl.pallas_call(make_kernel(rows, cols, ch, zrows, zcols, zch, hid, tr, nr...  22.3 us

profile of v2, /device:TPU:0, one launch (start us, length us, event | category | flops | bytes accessed | tf_op | source)
XLA Modules:
  0.0 50.4 jit_solution(4536541931972876048)
XLA Ops:
  0.6 22.3 %shard_map.220 = (f32[32,32]{1,0:T(8,128)}, bf16[1024,320]{1,0:T(8,128)(2,1)}, f32[64,192]{1,0:T(8,128)}) custom-call(s32[6]{0:T(128)} %refs_0_.1, bf16[1024,320]{1,0:T(8,128)(2,1)} %bitcast.8, bf16[64,192]{1,0:T(8,128)(2,1)} %bitcast.9, bf16[1728,192]{1,0:T(8,128)(2,1)} %bitcast.7, bf16[192,640]{1,0:T(8,128)(2,1)} %refs_4_.1, bf16[1280,640]{1,0:T(8,128)(2,1)} %bitcast.6, ...), custom_call_target="tpu_custom_call" | custom-call | tf_op jit(solution)/shard_map/pallas_call | solution.py:513
  22.9 27.5 %shard_map.221 = (f32[32,32]{1,0:T(8,128)}, bf16[1024,320]{1,0:T(8,128)(2,1)}, f32[64,192]{1,0:T(8,128)}) custom-call(f32[32,32]{1,0:T(8,128)} %get-tuple-element.9.rate, bf16[1024,320]{1,0:T(8,128)(2,1)} %get-tuple-element.10.gl, f32[64,192]{1,0:T(8,128)} %get-tuple-element.11.gh), custom_call_target="tpu_custom_call" | custom-call | tf_op jit(solution)/shard_map/pallas_call | solution.py:476

commit v3 on v2

--- a/solution.py
+++ b/solution.py
@@ -458,16 +458,21 @@
     return kernel
 
 
-def move(rate, gl, gh, rate_out, gl_out, gh_out, sem):
+def move(rate, gl, gh, rate_out, gl_out, gh_out, rate_v, gl_v, gh_v, sem, sem_out):
     parts = 4
     size = gl.shape[0] // parts
-    copies = [pltpu.make_async_copy(rate, rate_out, sem.at[0]), pltpu.make_async_copy(gh, gh_out, sem.at[1])]
+    triples = [(rate, rate_v, rate_out), (gh, gh_v, gh_out)]
     for i in range(parts):
         span = pl.ds(i * size, size)
-        copies.append(pltpu.make_async_copy(gl.at[span], gl_out.at[span], sem.at[2 + i]))
-    for c in copies:
+        triples.append((gl.at[span], gl_v.at[span], gl_out.at[span]))
+    ins = [pltpu.make_async_copy(a, b, sem.at[i]) for i, (a, b, _) in enumerate(triples)]
+    outs = [pltpu.make_async_copy(b, c, sem_out.at[i]) for i, (_, b, c) in enumerate(triples)]
+    for c in ins:
         c.start()
-    for c in copies:
+    for a, b in zip(ins, outs):
+        a.wait()
+        b.start()
+    for c in outs:
         c.wait()
 
 
@@ -478,7 +483,7 @@
         out_shape=tuple(jax.ShapeDtypeStruct(a.shape, a.dtype) for a in arrays),
         in_specs=[anyspec] * 3,
         out_specs=(anyspec,) * 3,
-        scratch_shapes=[pltpu.SemaphoreType.DMA((6,))],
+        scratch_shapes=[pltpu.VMEM(a.shape, a.dtype) for a in arrays] + [pltpu.SemaphoreType.DMA((6,))] * 2,
     )(*arrays)
 
 

time: 50.6 us -> 25.2 us (0.50)
  Pallas kernels: 49.8 us -> 24.3 us
    pallas_call x1, Pallas kernels: 27.5 us -> 2.05 us  [finish(): pl.pallas_call(move, out_shape=tuple((jax.ShapeDtypeStruct(a.shape, a.dty...]
where the time goes in v3:
time: 25.2 us; the launch traced here: 25 us
  Pallas kernels  24.3 us (96%)
  between operations  0.64 us (3%)
    pallas_call x1, Pallas kernels, local(): pl.pallas_call(make_kernel(rows, cols, ch, zrows, zcols, zch, hid, tr, nr...  22.3 us
    pallas_call x1, Pallas kernels, finish(): pl.pallas_call(move, out_shape=tuple((jax.ShapeDtypeStruct(a.shape, a.dty...  2.05 us

profile of v3, /device:TPU:0, one launch (start us, length us, event | category | flops | bytes accessed | tf_op | source)
XLA Modules:
  0.0 25.0 jit_solution(8227563069931440716)
XLA Ops:
  0.6 22.3 %shard_map.220 = (f32[32,32]{1,0:T(8,128)}, bf16[1024,320]{1,0:T(8,128)(2,1)}, f32[64,192]{1,0:T(8,128)}) custom-call(s32[6]{0:T(128)} %refs_0_.1, bf16[1024,320]{1,0:T(8,128)(2,1)} %bitcast.8, bf16[64,192]{1,0:T(8,128)(2,1)} %bitcast.9, bf16[1728,192]{1,0:T(8,128)(2,1)} %bitcast.7, bf16[192,640]{1,0:T(8,128)(2,1)} %refs_4_.1, bf16[1280,640]{1,0:T(8,128)(2,1)} %bitcast.6, ...), custom_call_target="tpu_custom_call" | custom-call | tf_op jit(solution)/shard_map/pallas_call | solution.py:518
  22.9 2.0 %shard_map.221 = (f32[32,32]{1,0:T(8,128)}, bf16[1024,320]{1,0:T(8,128)(2,1)}, f32[64,192]{1,0:T(8,128)}) custom-call(f32[32,32]{1,0:T(8,128)} %get-tuple-element.9.rate, bf16[1024,320]{1,0:T(8,128)(2,1)} %get-tuple-element.10.gl, f32[64,192]{1,0:T(8,128)} %get-tuple-element.11.gh), custom_call_target="tpu_custom_call" | custom-call | tf_op jit(solution)/shard_map/pallas_call | solution.py:481

commit v4 on v3

--- a/solution.py
+++ b/solution.py
@@ -233,6 +233,11 @@
         for i in ld_early:
             loads[i].wait()
         csh[...] = dot(ez[...], he[pl.ds(0, cells), :]).astype(BF)
+        count = jnp.int32(0)
+        for d in range(8):
+            count = count + there(d).astype(jnp.int32)
+        pl.semaphore_wait(barrier, count)
+        start(hyper_c)
         n8 = 8 * half
         for t in range(rows // 8):
             y = dot(ps[...], lat[pl.ds(t * 8 * cols, 8 * cols), :])
@@ -242,11 +247,6 @@
             ss[pl.ds(t * n8, n8), :] = y[2 * n8 :]
         csf[...] = dot(ef[...], ae[pl.ds(half, own), :]).astype(BF)
 
-        count = jnp.int32(0)
-        for d in range(8):
-            count = count + there(d).astype(jnp.int32)
-        pl.semaphore_wait(barrier, count)
-        start(hyper_c)
         start(lat_c)
 
         def ids(shape, dim, period, width):

time: 25.2 us -> 25 us (level)
  no operation moved by 1% of the time
where the time goes in v4:
time: 25 us; the launch traced here: 24.8 us
  Pallas kernels  24.1 us (96%)
  between operations  0.64 us (3%)
    pallas_call x1, Pallas kernels, local(): pl.pallas_call(make_kernel(rows, cols, ch, zrows, zcols, zch, hid, tr, nr...  22.1 us
    pallas_call x1, Pallas kernels, finish(): pl.pallas_call(move, out_shape=tuple((jax.ShapeDtypeStruct(a.shape, a.dty...  2.05 us

profile of v4, /device:TPU:0, one launch (start us, length us, event | category | flops | bytes accessed | tf_op | source)
XLA Modules:
  0.0 24.8 jit_solution(13667286067867526404)
XLA Ops:
  0.6 22.1 %shard_map.220 = (f32[32,32]{1,0:T(8,128)}, bf16[1024,320]{1,0:T(8,128)(2,1)}, f32[64,192]{1,0:T(8,128)}) custom-call(s32[6]{0:T(128)} %refs_0_.1, bf16[1024,320]{1,0:T(8,128)(2,1)} %bitcast.8, bf16[64,192]{1,0:T(8,128)(2,1)} %bitcast.9, bf16[1728,192]{1,0:T(8,128)(2,1)} %bitcast.7, bf16[192,640]{1,0:T(8,128)(2,1)} %refs_4_.1, bf16[1280,640]{1,0:T(8,128)(2,1)} %bitcast.6, ...), custom_call_target="tpu_custom_call" | custom-call | tf_op jit(solution)/shard_map/pallas_call | solution.py:518
  22.7 2.0 %shard_map.221 = (f32[32,32]{1,0:T(8,128)}, bf16[1024,320]{1,0:T(8,128)(2,1)}, f32[64,192]{1,0:T(8,128)}) custom-call(f32[32,32]{1,0:T(8,128)} %get-tuple-element.9.rate, bf16[1024,320]{1,0:T(8,128)(2,1)} %get-tuple-element.10.gl, f32[64,192]{1,0:T(8,128)} %get-tuple-element.11.gh), custom_call_target="tpu_custom_call" | custom-call | tf_op jit(solution)/shard_map/pallas_call | solution.py:481
